TPU v7x, 32 devices: a whole 2x2x4 slice. The times are simulated.
32 devices in a mesh: groups: 2 (over y), loop: 4 (over z), hid: 4 (over x, core).
Axes of the slice: x: 2, y: 2, z: 4, core: 2. Of those that a mesh axis runs over, the one named last changes fastest.
Arguments:
- tokens: bfloat16 [2048, 2048], P(('groups', 'loop')), parts along dimension 0, may hold values from -6 to 6
- route_ids: int32 [2048, 8], P(('groups', 'loop')), parts along dimension 0, may hold values from 0 to 127, all different within a row; in each aligned block of 256 rows (0 to 255, 256 to 511, ...) at most 32 rows name the same one
- router_weights: float32 [2048, 8], P(('groups', 'loop')), parts along dimension 0, may hold values from 1 to 3
- accepted: int32 [2048], P(('groups', 'loop')), parts along dimension 0, may hold values 0 or 1
- parents: int32 [2048], P(('groups', 'loop')), parts along dimension 0, may hold values from 0 to 62, as said below
- expert_weights: bfloat16 [4, 3, 1536, 2048], P(None, None, 'hid', 'loop'), may hold values from -0.125 to 0.125
Outputs:
- expert_out: bfloat16 [2048, 2048], P(('groups', 'loop'), 'hid'), parts along dimension 0
- parent_out: bfloat16 [2048, 2048], P(('groups', 'loop'), 'hid'), parts along dimension 0
There are 2 independent parts, one for each index of `groups`. A program takes and returns all parts, laid end to end along the dimension named above; an argument that names none is the same for every part. Nothing has to cross between parts.
Inputs may be any that keep to these rules, and one draw needn't show every extreme that they name: `route_ids`: the 8 ids of a row are different; no expert is named by more than 32 of the rows of one index of loop, a bound that some block reaches. `parents`: A node's parent is an earlier node of the same tree; the first node of a tree is its own parent, and the last node's parent is the node just before it.
All inputs are finite; a program needn't handle non-finite values. No bound on the sum of `accepted` on one device may be relied on, other than what follows from the above.
Results may differ from a plain program's by a relative error of at most 0.005.
Values may be sent and summed in bfloat16 or wider, within the bound.
A program may use at most 64 MiB of HBM per device.

v0:
```python
import jax
import jax.numpy as jnp
from jax import lax
from jax.sharding import PartitionSpec as P

NODES = 64


def shifted(value, axis, by):
    devices = lax.axis_size(axis)
    return lax.ppermute(value, axis, [(i, (i + by) % devices) for i in range(devices)])


def move_one(piece, phase_name):
    if phase_name == "proj":
        return shifted(piece, "loop", 1)
    return shifted(piece, "loop", 1)


def rotate(piece, start_value, add_piece, phase_name):
    n_loop = lax.axis_size("loop")
    own_index = lax.axis_index("loop")
    total = add_piece(start_value, piece, own_index)

    def turn_body(turn_no, carried):
        arrived = move_one(carried[0], phase_name)
        anchor = jnp.mod(own_index - turn_no, n_loop)
        return (arrived, add_piece(carried[1], arrived, anchor))

    carried = lax.fori_loop(1, n_loop, turn_body, (piece, total))
    return carried[1]


def local(tokens, route_ids, router_weights, accepted, parents, expert_weights):
    row_count = tokens.shape[0]
    model_width = tokens.shape[1]
    window_count = expert_weights.shape[0]
    hidden_share = expert_weights.shape[2]
    slab_width = expert_weights.shape[3]
    proj_weights = expert_weights[:, 0:2]
    down_weights = expert_weights[:, 2]
    matches = route_ids[:, :, None] == jnp.arange(window_count, dtype=jnp.int32)[None, None, :]
    live_rows = accepted > 0
    combine = jnp.where(
        live_rows[:, None],
        jnp.sum(jnp.where(matches, router_weights[:, :, None], 0.0), axis=1),
        0.0,
    )

    def proj_piece(total, piece, anchor):
        columns = lax.dynamic_slice_in_dim(tokens, anchor * slab_width, slab_width, 1)
        return total + jnp.einsum(
            "rd,etfd->retf", columns, piece, preferred_element_type=jnp.float32
        )

    proj_start = jnp.zeros((row_count, window_count, 2, hidden_share), jnp.float32)
    projected = rotate(proj_weights, proj_start, proj_piece, "proj")
    weighted = (combine[:, :, None] * jax.nn.silu(projected[:, :, 0]) * projected[:, :, 1]).astype(
        jnp.bfloat16
    )

    def down_piece(total, piece, anchor):
        block = jnp.einsum("ref,efd->rd", weighted, piece, preferred_element_type=jnp.float32)
        return lax.dynamic_update_slice_in_dim(total, block, anchor * slab_width, 1)

    partial_value = rotate(
        down_weights, jnp.zeros((row_count, model_width), jnp.float32), down_piece, "down"
    )
    share_width = model_width // lax.axis_size("hid")
    summed_all = lax.psum(partial_value, "hid")
    expert_out = lax.dynamic_slice_in_dim(
        summed_all, lax.axis_index("hid") * share_width, share_width, 1
    ).astype(jnp.bfloat16)
    tree_count = row_count // NODES
    family = jax.nn.one_hot(parents.reshape(tree_count, NODES), NODES, dtype=jnp.bfloat16)
    grouped = expert_out.reshape(tree_count, NODES, share_width)
    parent_out = jnp.einsum("qnm,qmd->qnd", family, grouped, preferred_element_type=jnp.float32)
    parent_out = parent_out.astype(jnp.bfloat16).reshape(row_count, share_width)
    return (expert_out, parent_out)


def solution(mesh):
    in_specs = (
        P(("groups", "loop"), None),
        P(("groups", "loop"), None),
        P(("groups", "loop"), None),
        P(("groups", "loop")),
        P(("groups", "loop")),
        P(None, None, "hid", "loop"),
    )
    out_specs = (P(("groups", "loop"), "hid"), P(("groups", "loop"), "hid"))
    return jax.shard_map(local, mesh=mesh, in_specs=in_specs, out_specs=out_specs, check_vma=False)
```

profile of v0, /device:TPU:3, one launch (start us, length us, event | category | flops | bytes accessed | tf_op | source)
XLA Modules:
  0.0 399.5 jit_solution(2713133171892868175)
XLA Ops:
  0.6 4.8 %fusion.12 = f32[256,4,2,384]{3,0,2,1:T(8,128)} fusion(bf16[256,2048]{1,0:T(8,128)(2,1)} %param.10, s32[]{:T(128)S(6)} %select_n.78, bf16[4,3,384,512]{3,2,1,0:T(8,128)(2,1)} %param.15), kind=kOutput, calls=%fused_computation.22 | convolution fusion | flops 805306368 | bytes 6553604 | tf_op jit(solution)/shard_map/rd,etfd->retf/dot_general | solution.py:52
  5.5 1.8 slice.13
  7.3 227.3 %while.34 = (s32[]{:T(128)}, bf16[4,2,384,512]{3,2,1,0:T(8,128)(2,1)}, f32[256,4,2,384]{3,0,2,1:T(8,128)}, s32[]{:T(128)}, bf16[256,2048]{1,0:T(8,128)(2,1)}, /*...) while((s32[]{:T(128)}, bf16[4,2,384,512]{3,2,1,0:T(8,128)(2,1)}, ...), condition=%wide.region_2.3_spmd, body=%wide.region_1.2_spmd.sunk | while | flops 806092800 | bytes 53739888 | solution.py:30
  7.3 1.3 collective-permute-start
  8.6 69.8 %collective-permute-done = bf16[4,2,384,512]{3,2,1,0:T(8,128)(2,1)S(1)} collective-permute-done((bf16[4,2,384,512]{3,2,1,0:T(8,128)(2,1)}, bf16[4,2,384,512]{3,2,1,0:T(8,128)(2,1)S(1)}, u32[]{:S(2)}, u32[]{:S(2)}) %collective-permute-start) | collective-permute-done | bytes 3145760 | tf_op jit(solution)/shard_map/while/body/eval_jaxpr/ppermute | solution.py:11
  78.4 1.6 copy.32
  80.1 2.3 convolution_add_fusion.2
  82.4 1.7 copy-done.1
  84.0 70.1 %collective-permute-done = bf16[4,2,384,512]{3,2,1,0:T(8,128)(2,1)S(1)} collective-permute-done((bf16[4,2,384,512]{3,2,1,0:T(8,128)(2,1)}, bf16[4,2,384,512]{3,2,1,0:T(8,128)(2,1)S(1)}, u32[]{:S(2)}, u32[]{:S(2)}) %collective-permute-start) | collective-permute-done | bytes 3145760 | tf_op jit(solution)/shard_map/while/body/eval_jaxpr/ppermute | solution.py:11
  154.2 1.6 copy.32
  155.8 2.3 convolution_add_fusion.2
  158.1 1.7 copy-done.1
  159.8 69.2 %collective-permute-done = bf16[4,2,384,512]{3,2,1,0:T(8,128)(2,1)S(1)} collective-permute-done((bf16[4,2,384,512]{3,2,1,0:T(8,128)(2,1)}, bf16[4,2,384,512]{3,2,1,0:T(8,128)(2,1)S(1)}, u32[]{:S(2)}, u32[]{:S(2)}) %collective-permute-start) | collective-permute-done | bytes 3145760 | tf_op jit(solution)/shard_map/while/body/eval_jaxpr/ppermute | solution.py:11
  229.0 1.6 copy.32
  230.6 2.3 convolution_add_fusion.2
  232.9 1.7 copy-done.1
  234.6 1.6 broadcast_in_dim.34
  236.2 4.0 fusion.9
  240.2 0.5 fusion.4
  240.7 2.7 slice_bitcast_fusion
  243.4 108.6 %while.35 = (s32[]{:T(128)}, bf16[4,384,512]{2,1,0:T(8,128)(2,1)}, f32[256,2048]{1,0:T(8,128)}, bf16[256,4,384]{2,0,1:T(8,128)(2,1)S(1)}, s32[]{:T(128)}, /*inde...) while((s32[]{:T(128)}, bf16[4,384,512]{2,1,0:T(8,128)(2,1)}, ...), condition=%wide.region_4.5_spmd, body=%wide.region_3.4_spmd.sunk | while | flops 402653216 | bytes 12321088 | solution.py:30
  243.4 34.6 %collective-permute-done.1 = bf16[4,384,512]{2,1,0:T(8,128)(2,1)S(1)} collective-permute-done((bf16[4,384,512]{2,1,0:T(8,128)(2,1)}, bf16[4,384,512]{2,1,0:T(8,128)(2,1)S(1)}, u32[]{:S(2)}, u32[]{:S(2)}) %collective-permute-start.1) | collective-permute-done | bytes 1572896 | tf_op jit(solution)/shard_map/while/body/eval_jaxpr/ppermute | solution.py:11
  277.9 1.1 copy.42
  279.1 1.4 fusion.34
  280.5 33.7 %collective-permute-done.1 = bf16[4,384,512]{2,1,0:T(8,128)(2,1)S(1)} collective-permute-done((bf16[4,384,512]{2,1,0:T(8,128)(2,1)}, bf16[4,384,512]{2,1,0:T(8,128)(2,1)S(1)}, u32[]{:S(2)}, u32[]{:S(2)}) %collective-permute-start.1) | collective-permute-done | bytes 1572896 | tf_op jit(solution)/shard_map/while/body/eval_jaxpr/ppermute | solution.py:11
  314.1 1.1 copy.42
  315.3 1.4 fusion.34
  316.7 32.7 %collective-permute-done.1 = bf16[4,384,512]{2,1,0:T(8,128)(2,1)S(1)} collective-permute-done((bf16[4,384,512]{2,1,0:T(8,128)(2,1)}, bf16[4,384,512]{2,1,0:T(8,128)(2,1)S(1)}, u32[]{:S(2)}, u32[]{:S(2)}) %collective-permute-start.1) | collective-permute-done | bytes 1572896 | tf_op jit(solution)/shard_map/while/body/eval_jaxpr/ppermute | solution.py:11
  349.5 1.1 copy.42
  350.6 1.4 fusion.34
  352.0 46.4 %all-reduce.1 = bf16[256,2048]{1,0:T(8,128)(2,1)S(1)} all-reduce(f32[256,2048]{1,0:T(8,128)} %get-tuple-element.269), channel_id=1, replica_groups=mesh['groups'=2,'loop'=4,'hid'=4] {'hid'}, use_global_device_ids=true, to_apply=%region_5.6 | all-reduce | flops 524288 | bytes 3145728 | tf_op jit(solution)/shard_map/psum | solution.py:70
  398.5 1.0 convolution_convert_fusion
  (33 shorter events, 0.2 us)
Async XLA Ops:
  0.6 4.8 %copy-start.3 = (bf16[4,3,384,512]{3,2,1,0:T(8,128)(2,1)S(1)}, bf16[4,3,384,512]{3,2,1,0:T(8,128)(2,1)}, u32[]{:S(2)}) copy-start(bf16[4,3,384,512]{3,2,1,0:T(8,128)(2,1)} %param.15) | copy-start | bytes 14155780
  7.3 227.3 %copy-start.5 = (f32[256,8]{0,1:T(8,128)S(1)}, f32[256,8]{0,1:T(8,128)}, u32[]{:S(2)}) copy-start(f32[256,8]{0,1:T(8,128)} %param.12) | copy-start | bytes 24580
  7.3 227.3 %copy-start.6 = (s32[256,8]{0,1:T(8,128)S(1)}, s32[256,8]{0,1:T(8,128)}, u32[]{:S(2)}) copy-start(s32[256,8]{0,1:T(8,128)} %param.11) | copy-start | bytes 24580
  7.3 227.3 %copy-start.8 = (s32[256]{0:T(256)S(1)}, s32[256]{0:T(256)}, u32[]{:S(2)}) copy-start(s32[256]{0:T(256)} %param.13) | copy-start | bytes 3076
  7.3 71.1 %collective-permute-start = (bf16[4,2,384,512]{3,2,1,0:T(8,128)(2,1)}, bf16[4,2,384,512]{3,2,1,0:T(8,128)(2,1)S(1)}, u32[]{:S(2)}, u32[]{:S(2)}) collective-permute-start(bf16[4,2,384,512]{3,2,1,0:T(8,128)(2,1)} %get-tuple-element.364), channel_id=1, source_target_pairs={{0,4},{4,8},{8,12},{12,0},{1,5},{5,9},{9,13},{13,1},{2,6},{6,10},{... | collective-permute-start | bytes 9437192 | tf_op jit(solution)/shard_map/while/body/eval_jaxpr/ppermute | solution.py:11
  8.6 71.5 %copy-start = (f32[256,4,2,384]{3,0,2,1:T(8,128)S(1)}, f32[256,4,2,384]{3,0,2,1:T(8,128)}, u32[]{:S(2)}) copy-start(f32[256,4,2,384]{3,0,2,1:T(8,128)} %get-tuple-element.365) | copy-start | bytes 9437188 | tf_op jit(solution)/shard_map/while
  82.4 1.7 copy-start.1
  84.0 70.1 %collective-permute-start = (bf16[4,2,384,512]{3,2,1,0:T(8,128)(2,1)}, bf16[4,2,384,512]{3,2,1,0:T(8,128)(2,1)S(1)}, u32[]{:S(2)}, u32[]{:S(2)}) collective-permute-start(bf16[4,2,384,512]{3,2,1,0:T(8,128)(2,1)} %get-tuple-element.364), channel_id=1, source_target_pairs={{0,4},{4,8},{8,12},{12,0},{1,5},{5,9},{9,13},{13,1},{2,6},{6,10},{... | collective-permute-start | bytes 9437192 | tf_op jit(solution)/shard_map/while/body/eval_jaxpr/ppermute | solution.py:11
  84.0 71.8 %copy-start = (f32[256,4,2,384]{3,0,2,1:T(8,128)S(1)}, f32[256,4,2,384]{3,0,2,1:T(8,128)}, u32[]{:S(2)}) copy-start(f32[256,4,2,384]{3,0,2,1:T(8,128)} %get-tuple-element.365) | copy-start | bytes 9437188 | tf_op jit(solution)/shard_map/while
  158.1 1.7 copy-start.1
  159.8 69.2 %collective-permute-start = (bf16[4,2,384,512]{3,2,1,0:T(8,128)(2,1)}, bf16[4,2,384,512]{3,2,1,0:T(8,128)(2,1)S(1)}, u32[]{:S(2)}, u32[]{:S(2)}) collective-permute-start(bf16[4,2,384,512]{3,2,1,0:T(8,128)(2,1)} %get-tuple-element.364), channel_id=1, source_target_pairs={{0,4},{4,8},{8,12},{12,0},{1,5},{5,9},{9,13},{13,1},{2,6},{6,10},{... | collective-permute-start | bytes 9437192 | tf_op jit(solution)/shard_map/while/body/eval_jaxpr/ppermute | solution.py:11
  159.8 70.9 %copy-start = (f32[256,4,2,384]{3,0,2,1:T(8,128)S(1)}, f32[256,4,2,384]{3,0,2,1:T(8,128)}, u32[]{:S(2)}) copy-start(f32[256,4,2,384]{3,0,2,1:T(8,128)} %get-tuple-element.365) | copy-start | bytes 9437188 | tf_op jit(solution)/shard_map/while
  232.9 1.7 copy-start.1
  236.2 4.0 copy-start.2
  243.4 34.6 %collective-permute-start.1 = (bf16[4,384,512]{2,1,0:T(8,128)(2,1)}, bf16[4,384,512]{2,1,0:T(8,128)(2,1)S(1)}, u32[]{:S(2)}, u32[]{:S(2)}) collective-permute-start(bf16[4,384,512]{2,1,0:T(8,128)(2,1)} %get-tuple-element.397), channel_id=1, source_target_pairs={{0,4},{4,8},{8,12},{12,0},{1,5},{5,9},{9,13},{13,1},{2,6},{6,10},{... | collective-permute-start | bytes 4718600 | tf_op jit(solution)/shard_map/while/body/eval_jaxpr/ppermute | solution.py:11
  280.5 33.7 %collective-permute-start.1 = (bf16[4,384,512]{2,1,0:T(8,128)(2,1)}, bf16[4,384,512]{2,1,0:T(8,128)(2,1)S(1)}, u32[]{:S(2)}, u32[]{:S(2)}) collective-permute-start(bf16[4,384,512]{2,1,0:T(8,128)(2,1)} %get-tuple-element.397), channel_id=1, source_target_pairs={{0,4},{4,8},{8,12},{12,0},{1,5},{5,9},{9,13},{13,1},{2,6},{6,10},{... | collective-permute-start | bytes 4718600 | tf_op jit(solution)/shard_map/while/body/eval_jaxpr/ppermute | solution.py:11
  316.7 32.7 %collective-permute-start.1 = (bf16[4,384,512]{2,1,0:T(8,128)(2,1)}, bf16[4,384,512]{2,1,0:T(8,128)(2,1)S(1)}, u32[]{:S(2)}, u32[]{:S(2)}) collective-permute-start(bf16[4,384,512]{2,1,0:T(8,128)(2,1)} %get-tuple-element.397), channel_id=1, source_target_pairs={{0,4},{4,8},{8,12},{12,0},{1,5},{5,9},{9,13},{13,1},{2,6},{6,10},{... | collective-permute-start | bytes 4718600 | tf_op jit(solution)/shard_map/while/body/eval_jaxpr/ppermute | solution.py:11
  352.0 46.5 %copy-start.7 = (s32[256]{0:T(256)S(1)}, s32[256]{0:T(256)}, u32[]{:S(2)}) copy-start(s32[256]{0:T(256)} %param.14) | copy-start | bytes 3076
  398.4 1.1 copy-start.4
where the time goes:
time: 403 us; the launch traced here: 400 us
  waiting for transfers between devices  310 us (77%)
  blocking collectives  46.4 us (12%)
  matrix products  20.8 us (5%)
  local copies, waits for them, and re-layouts  19.6 us (5%)
    ppermute x6, waiting for transfers between devices, shifted(): lax.ppermute(value, axis, [(i, (i + by) % devices) for i in range(devices)])  310 us
    psum x1, blocking collectives, local(): summed_all = lax.psum(partial_value, 'hid')  46.4 us
    while x18, local copies, waits for them, and re-layouts  13.4 us
    dot_general x4, matrix products, proj_piece(): jnp.einsum('rd,etfd->retf', columns, piece, preferred_element_type=jnp.fl...  11.6 us
    dot_general x4, matrix products, down_piece(): jnp.einsum('ref,efd->rd', weighted, piece, preferred_element_type=jnp.flo...  8.17 us
  transfers between devices with their start and end apart: 6, of which 6 were waited for; matrix products, arithmetic and copies ran while one was open for 0% of the time, Pallas kernels for 0%

commit v1 on v0

--- a/solution.py
+++ b/solution.py
@@ -1,9 +1,236 @@
+import functools
+
 import jax
 import jax.numpy as jnp
 from jax import lax
+from jax.experimental import pallas as pl
+from jax.experimental.pallas import tpu as pltpu
 from jax.sharding import PartitionSpec as P
 
 NODES = 64
+CAP = 32
+MESH = pl.DeviceIdType.MESH
+
+
+def moe_kernel(
+    n, ids_ref, rw_ref, acc_ref, par_ref, tok_ref, w_hbm, out_ref, pout_ref,
+    w, xsend, xbuf, psend, pbuf, hbuf, fsend, fin,
+    w_sem, xs_sem, xr_sem, ps_sem, pr_sem, hs_sem, hr_sem, fs_sem, fr_sem,
+):
+    me = lax.axis_index("loop")
+    hid = lax.axis_index("hid")
+    rows, width = tok_ref.shape
+    experts, _, share, slab = w.shape
+    slots = experts * CAP
+    on_diag = me == hid
+
+    def plus(k):
+        return lax.rem(me + k, n)
+
+    def minus(k):
+        return lax.rem(me + n - k, n)
+
+    barrier = pltpu.get_barrier_semaphore()
+    for k in range(1, n):
+        pl.semaphore_signal(barrier, inc=1, device_id={"loop": plus(k)}, device_id_type=MESH)
+    for k in range(1, n):
+        pl.semaphore_signal(
+            barrier, inc=1, device_id={"loop": hid, "hid": lax.rem(hid + k, n)}, device_id_type=MESH
+        )
+
+    @pl.when(jnp.logical_not(on_diag))
+    def _():
+        pl.semaphore_signal(barrier, inc=1, device_id={"loop": hid, "hid": hid}, device_id_type=MESH)
+
+    w_copies = [pltpu.make_async_copy(w_hbm.at[e], w.at[e], w_sem.at[e]) for e in range(experts)]
+    for copy in w_copies:
+        copy.start()
+
+    f32, bf16 = jnp.float32, jnp.bfloat16
+    r_i = lax.broadcasted_iota(jnp.int32, (rows, rows), 0)
+    c_i = lax.broadcasted_iota(jnp.int32, (rows, rows), 1)
+    eye = r_i == c_i
+    acc = jnp.sum(jnp.where(eye, acc_ref[...].astype(f32), 0.0), axis=1, keepdims=True)
+    live = acc > 0.0
+    ids = ids_ref[...]
+    rw = rw_ref[...]
+    lane = lax.broadcasted_iota(jnp.int32, (rows, slots), 1)
+    lane_e = lane // CAP
+    lane_i = (lane - lane_e * CAP).astype(f32)
+    match = jnp.zeros((rows, slots), f32)
+    factor = jnp.zeros((rows, slots), f32)
+    for e in range(experts):
+        hit = (ids == e) & live
+        m_e = jnp.sum(jnp.where(hit, 1.0, 0.0), axis=1, keepdims=True)
+        f_e = jnp.sum(jnp.where(hit, rw, 0.0), axis=1, keepdims=True)
+        match = jnp.where(lane_e == e, m_e, match)
+        factor = jnp.where(lane_e == e, f_e, factor)
+    lower = jnp.where(c_i < r_i, 1.0, 0.0).astype(bf16)
+    rank = jnp.dot(lower, match.astype(bf16), preferred_element_type=f32)
+    picked = (match > 0.0) & (rank == lane_i)
+    place = jnp.where(picked, 1.0, 0.0)
+    place_t = jnp.transpose(place).astype(bf16)
+    factor_row = jnp.sum(jnp.where(picked, factor, 0.0), axis=0, keepdims=True)
+    s_r = lax.broadcasted_iota(jnp.int32, (slots, slots), 0)
+    s_c = lax.broadcasted_iota(jnp.int32, (slots, slots), 1)
+    factor_col = jnp.sum(jnp.where(s_r == s_c, factor_row, 0.0), axis=1, keepdims=True)
+
+    for k in range(n):
+        cols = pl.ds(pl.multiple_of(plus(k) * slab, slab), slab)
+        chosen = jnp.dot(place_t, tok_ref[:, cols], preferred_element_type=f32).astype(bf16)
+        target = xbuf if k == 0 else xsend
+        target[k if k == 0 else k - 1] = chosen.reshape(experts, CAP, slab)
+
+    @pl.when(on_diag)
+    def _():
+        pl.semaphore_wait(barrier, 2 * (n - 1))
+
+    @pl.when(jnp.logical_not(on_diag))
+    def _():
+        pl.semaphore_wait(barrier, 2 * (n - 1) + 1)
+
+    def x_copy(k, e):
+        return pltpu.make_async_remote_copy(
+            src_ref=xsend.at[k - 1, e], dst_ref=xbuf.at[k, e],
+            send_sem=xs_sem.at[k - 1, e], recv_sem=xr_sem.at[k - 1, e],
+            device_id={"loop": plus(k)}, device_id_type=MESH,
+        )
+
+    def p_copy(k, e):
+        return pltpu.make_async_remote_copy(
+            src_ref=psend.at[e, k], dst_ref=pbuf.at[k - 1, e],
+            send_sem=ps_sem.at[k - 1, e], recv_sem=pr_sem.at[k - 1, e],
+            device_id={"loop": minus(k)}, device_id_type=MESH,
+        )
+
+    def h_copy(k, e):
+        return pltpu.make_async_remote_copy(
+            src_ref=hbuf.at[e, 0], dst_ref=hbuf.at[e, k],
+            send_sem=hs_sem.at[k - 1, e], recv_sem=hr_sem.at[k - 1, e],
+            device_id={"loop": plus(k)}, device_id_type=MESH,
+        )
+
+    def f_copy(k, e, source):
+        return pltpu.make_async_remote_copy(
+            src_ref=fsend.at[e, k], dst_ref=fin.at[source, e],
+            send_sem=fs_sem.at[k, e], recv_sem=fr_sem.at[source, e],
+            device_id={"loop": minus(k), "hid": me}, device_id_type=MESH,
+        )
+
+    others = list(range(1, n))
+    for e in range(experts):
+        for k in others:
+            x_copy(k, e).start()
+
+    for e in range(experts):
+        w_copies[e].wait()
+        for k in others:
+            x_copy(k, e).wait_recv()
+        part = lax.dot_general(
+            xbuf[:, e].reshape(n * CAP, slab), w[e, 0:2].reshape(2 * share, slab),
+            (((1,), (1,)), ((), ())), preferred_element_type=f32,
+        )
+        psend[e] = part.reshape(n, CAP, 2 * share)
+        for k in others:
+            p_copy(k, e).start()
+
+    for e in range(experts):
+        for k in others:
+            p_copy(k, e).wait_recv()
+        total = psend[e, 0]
+        for k in others:
+            total = total + pbuf[k - 1, e]
+        gate, up = total[:, :share], total[:, share:]
+        col = factor_col[e * CAP:(e + 1) * CAP]
+        hbuf[e, 0] = (col * (gate / (1.0 + jnp.exp(-gate))) * up).astype(bf16)
+        for k in others:
+            h_copy(k, e).start()
+
+    for e in range(experts):
+        for k in others:
+            h_copy(k, e).wait_recv()
+        block = jnp.dot(
+            hbuf[e].reshape(n * CAP, share), w[e, 2], preferred_element_type=f32
+        ).astype(bf16).reshape(n, CAP, slab)
+        fsend[e] = block
+        for k in others:
+            f_copy(k, e, hid).start()
+
+        @pl.when(on_diag)
+        def _():
+            fin[hid, e] = block[0]
+
+        @pl.when(jnp.logical_not(on_diag))
+        def _():
+            f_copy(0, e, hid).start()
+
+    base = r_i // NODES * NODES
+    par = jnp.sum(jnp.where(eye, par_ref[...].astype(f32), 0.0), axis=1, keepdims=True)
+    family = jnp.where((c_i - base).astype(f32) == par, 1.0, 0.0).astype(bf16)
+    place16 = place.astype(bf16)
+
+    for source in range(n):
+        @pl.when(jnp.logical_not(on_diag & (hid == source)))
+        def _():
+            for e in range(experts):
+                f_copy(1, e, source).wait_recv()
+
+    total = fin[0].astype(f32)
+    for source in range(1, n):
+        total = total + fin[source].astype(f32)
+    total = total.reshape(slots, slab)
+    high = total.astype(bf16)
+    low = (total - high.astype(f32)).astype(bf16)
+    value = jnp.dot(place16, high, preferred_element_type=f32) + jnp.dot(
+        place16, low, preferred_element_type=f32
+    )
+    value = value.astype(bf16)
+    out_ref[...] = value
+    pout_ref[...] = jnp.dot(family, value, preferred_element_type=f32).astype(bf16)
+
+    for e in range(experts):
+        for k in others:
+            x_copy(k, e).wait_send()
+            p_copy(k, e).wait_send()
+            h_copy(k, e).wait_send()
+            f_copy(k, e, hid).wait_send()
+
+        @pl.when(jnp.logical_not(on_diag))
+        def _():
+            f_copy(0, e, hid).wait_send()
+
+
+def compact(tokens, route_ids, router_weights, accepted, parents, expert_weights):
+    n = lax.axis_size("loop")
+    rows = tokens.shape[0]
+    experts, _, share, slab = expert_weights.shape
+    bf16, f32 = jnp.bfloat16, jnp.float32
+    vmem = pl.BlockSpec(memory_space=pltpu.VMEM)
+    dma = pltpu.SemaphoreType.DMA
+    return pl.pallas_call(
+        functools.partial(moe_kernel, n),
+        out_shape=[jax.ShapeDtypeStruct((rows, slab), bf16)] * 2,
+        in_specs=[vmem] * 5 + [pl.BlockSpec(memory_space=pl.ANY)],
+        out_specs=[vmem] * 2,
+        scratch_shapes=[
+            pltpu.VMEM(expert_weights.shape, bf16),
+            pltpu.VMEM((n - 1, experts, CAP, slab), bf16),
+            pltpu.VMEM((n, experts, CAP, slab), bf16),
+            pltpu.VMEM((experts, n, CAP, 2 * share), f32),
+            pltpu.VMEM((n - 1, experts, CAP, 2 * share), f32),
+            pltpu.VMEM((experts, n, CAP, share), bf16),
+            pltpu.VMEM((experts, n, CAP, slab), bf16),
+            pltpu.VMEM((n, experts, CAP, slab), bf16),
+            dma((experts,)),
+            dma((n - 1, experts)), dma((n - 1, experts)),
+            dma((n - 1, experts)), dma((n - 1, experts)),
+            dma((n - 1, experts)), dma((n - 1, experts)),
+            dma((n, experts)), dma((n, experts)),
+        ],
+        compiler_params=pltpu.CompilerParams(
+            collective_id=0, has_side_effects=True, vmem_limit_bytes=40 << 20
+        ),
+    )(route_ids, router_weights, accepted.reshape(1, rows), parents.reshape(1, rows), tokens, expert_weights)
 
 
 def shifted(value, axis, by):
@@ -31,7 +258,7 @@
     return carried[1]
 
 
-def local(tokens, route_ids, router_weights, accepted, parents, expert_weights):
+def general(tokens, route_ids, router_weights, accepted, parents, expert_weights):
     row_count = tokens.shape[0]
     model_width = tokens.shape[1]
     window_count = expert_weights.shape[0]
@@ -79,6 +306,15 @@
     return (expert_out, parent_out)
 
 
+def local(tokens, route_ids, router_weights, accepted, parents, expert_weights):
+    args = (tokens, route_ids, router_weights, accepted, parents, expert_weights)
+    experts, _, share, slab = expert_weights.shape
+    n_loop, n_hid = lax.axis_size("loop"), lax.axis_size("hid")
+    if n_loop == n_hid and slab % 128 == 0 and share % 128 == 0 and experts * CAP == 128:
+        return tuple(compact(*args))
+    return general(*args)
+
+
 def solution(mesh):
     in_specs = (
         P(("groups", "loop"), None),

time: 403 us -> 81.2 us (0.20)
  the two profiles are of different devices: /device:TPU:3 before, /device:TPU:2 now
where the time goes in v1:
time: 81.2 us; the launch traced here: 80.9 us
  Pallas kernels  72.3 us (89%)
  local copies, waits for them, and re-layouts  7.96 us (10%)
    pallas_call x1, Pallas kernels, compact(): pl.pallas_call(functools.partial(moe_kernel, n), out_shape=[jax.ShapeDtyp...  72.3 us
    unnamed x12, local copies, waits for them, and re-layouts  7.96 us

profile of v1, /device:TPU:2, one launch (start us, length us, event | category | flops | bytes accessed | tf_op | source)
XLA Modules:
  0.0 80.9 jit_solution(677640077956230965)
XLA Ops:
  0.6 0.8 %copy.8.ids_ref = s32[256,8]{1,0:T(8,128)S(1)} copy(s32[256,8]{0,1:T(8,128)} %param.7) | data formatting | bytes 16384 | tf_op args[1]
  1.5 0.8 %copy.9.rw_ref = f32[256,8]{1,0:T(8,128)S(1)} copy(f32[256,8]{0,1:T(8,128)} %param.8) | data formatting | bytes 16384 | tf_op args[2]
  2.3 0.0 copy-start
  2.3 2.3 %copy-done = bf16[4,3,384,512]{3,2,1,0:T(8,128)(2,1)S(1)} copy-done((bf16[4,3,384,512]{3,2,1,0:T(8,128)(2,1)S(1)}, bf16[4,3,384,512]{3,2,1,0:T(8,128)(2,1)}, u32[]{:S(2)}) %copy-start) | copy-done | bytes 4718616
  4.6 0.0 copy-start.1
  4.6 1.2 %copy-done.1 = bf16[256,2048]{1,0:T(8,128)(2,1)S(1)} copy-done((bf16[256,2048]{1,0:T(8,128)(2,1)S(1)}, bf16[256,2048]{1,0:T(8,128)(2,1)}, u32[]{:S(2)}) %copy-start.1) | copy-done | bytes 1048600
  5.9 0.0 copy-start.2
  5.9 0.7 copy-done.2
  6.5 0.0 copy-start.3
  6.5 0.7 copy-done.3
  7.2 72.3 %shard_map.77 = (bf16[256,512]{1,0:T(8,128)(2,1)S(1)}, bf16[256,512]{1,0:T(8,128)(2,1)S(1)}) custom-call(s32[256,8]{1,0:T(8,128)S(1)} %copy.8.ids_ref, f32[256,8]{1,0:T(8,128)S(1)} %copy.9.rw_ref, s32[1,256]{1,0:T(1,128)S(1)} %bitcast.2, s32[1,256]{1,0:T(1,128)S(1)} %bitcast.3, bf16[256,2048]{1,0:T(8,128)(2,1)S(1)} %copy-done.1, ...), custom_call_target="tpu_custom_call" | custom-call | tf_op jit(solution)/shard_map/pallas_call | solution.py:210
  79.5 0.7 copy.12
  80.2 0.7 copy.13
Async XLA Ops:
  2.3 2.3 %copy-start = (bf16[4,3,384,512]{3,2,1,0:T(8,128)(2,1)S(1)}, bf16[4,3,384,512]{3,2,1,0:T(8,128)(2,1)}, u32[]{:S(2)}) copy-start(bf16[4,3,384,512]{3,2,1,0:T(8,128)(2,1)} %w_hbm.1) | copy-start | bytes 14155780
  4.6 1.2 %copy-start.1 = (bf16[256,2048]{1,0:T(8,128)(2,1)S(1)}, bf16[256,2048]{1,0:T(8,128)(2,1)}, u32[]{:S(2)}) copy-start(bf16[256,2048]{1,0:T(8,128)(2,1)} %tok_ref.1) | copy-start | bytes 3145732
  5.9 0.7 copy-start.2
  6.5 0.7 copy-start.3

commit v2 on v1

v2 whole, which is shorter than its diff:
```python
import functools

import jax
import jax.numpy as jnp
from jax import lax
from jax.experimental import pallas as pl
from jax.experimental.pallas import tpu as pltpu
from jax.sharding import PartitionSpec as P

NODES = 64
CAP = 32
MESH = pl.DeviceIdType.MESH
SENT = jnp.bfloat16


def moe_kernel(
    n, ids_hbm, rw_hbm, acc_hbm, par_hbm, tok_hbm, w_hbm, out_ref, pout_ref,
    ids_ref, rw_ref, acc_ref, par_ref, tok_ref, w,
    xsend, xbuf, pown, psend, pbuf, hbuf, fsend, rbuf, tsend, fin,
    in_sem, w_sem, xs_sem, xf_sem, xr_sem, ps_sem, pr_sem, hs_sem, hr_sem,
    rs_sem, rr_sem, ts_sem, tr_sem,
):
    me = lax.axis_index("loop")
    hid = lax.axis_index("hid")
    rows, width = tok_ref.shape
    experts, _, share, slab = w.shape
    slots = experts * CAP
    on_diag = me == hid
    others = list(range(1, n))

    def plus(index, k):
        return lax.rem(index + k, n)

    def minus(index, k):
        return lax.rem(index + n - k, n)

    barrier = pltpu.get_barrier_semaphore()
    for k in others:
        pl.semaphore_signal(barrier, inc=1, device_id={"loop": plus(me, k)}, device_id_type=MESH)
        pl.semaphore_signal(barrier, inc=1, device_id={"hid": plus(hid, k)}, device_id_type=MESH)

    @pl.when(jnp.logical_not(on_diag))
    def _():
        pl.semaphore_signal(barrier, inc=1, device_id={"loop": hid, "hid": me}, device_id_type=MESH)

    inputs = [
        pltpu.make_async_copy(source, target, in_sem.at[i])
        for i, (source, target) in enumerate(
            [(ids_hbm, ids_ref), (rw_hbm, rw_ref), (acc_hbm, acc_ref), (par_hbm, par_ref), (tok_hbm, tok_ref)]
        )
    ]
    for copy in inputs:
        copy.start()
    w_copies = [pltpu.make_async_copy(w_hbm.at[e], w.at[e], w_sem.at[e]) for e in range(experts)]
    for copy in w_copies:
        copy.start()

    f32, bf16 = jnp.float32, jnp.bfloat16
    r_i = lax.broadcasted_iota(jnp.int32, (rows, rows), 0)
    c_i = lax.broadcasted_iota(jnp.int32, (rows, rows), 1)
    upper = jnp.where(r_i < c_i, 1.0, 0.0).astype(bf16)
    slot = lax.broadcasted_iota(jnp.int32, (slots, rows), 0)
    slot_e = slot // CAP
    slot_i = (slot - slot_e * CAP).astype(f32)
    for copy in inputs:
        copy.wait()
    live = acc_ref[...] > 0
    ids = ids_ref[...]
    rw = rw_ref[...]
    match = jnp.zeros((slots, rows), f32)
    factor = jnp.zeros((slots, rows), f32)
    for e in range(experts):
        hit = (ids == e) & live
        m_e = jnp.sum(jnp.where(hit, 1.0, 0.0), axis=0, keepdims=True)
        f_e = jnp.sum(jnp.where(hit, rw, 0.0), axis=0, keepdims=True)
        match = jnp.where(slot_e == e, m_e, match)
        factor = jnp.where(slot_e == e, f_e, factor)
    rank = jnp.dot(match.astype(bf16), upper, preferred_element_type=f32)
    picked = (match > 0.0) & (rank == slot_i)
    place_t = jnp.where(picked, 1.0, 0.0)
    factor_col = jnp.sum(jnp.where(picked, factor, 0.0), axis=1, keepdims=True)
    place_t16 = place_t.astype(bf16)

    for k in others + [0]:
        cols = pl.ds(pl.multiple_of(plus(me, k) * slab, slab), slab)
        chosen = jnp.dot(place_t16, tok_ref[:, cols], preferred_element_type=f32)
        chosen = chosen.astype(bf16).reshape(experts, CAP, slab)
        if k == 0:
            xbuf[0] = chosen
        else:
            xsend[k - 1] = chosen

    @pl.when(on_diag)
    def _():
        pl.semaphore_wait(barrier, 2 * (n - 1))

    @pl.when(jnp.logical_not(on_diag))
    def _():
        pl.semaphore_wait(barrier, 2 * (n - 1) + 1)

    def x_copy(k, e):
        return pltpu.make_async_remote_copy(
            src_ref=xsend.at[k - 1, e], dst_ref=xbuf.at[k, e],
            send_sem=xs_sem.at[k - 1], recv_sem=xr_sem.at[k - 1, e],
            device_id={"loop": plus(me, k)}, device_id_type=MESH,
        )

    def x_forward(k, j):
        return pltpu.make_async_remote_copy(
            src_ref=xbuf.at[k, hid], dst_ref=xbuf.at[k, hid],
            send_sem=xf_sem.at[k - 1, j - 1], recv_sem=xr_sem.at[k - 1, hid],
            device_id={"hid": plus(hid, j)}, device_id_type=MESH,
        )

    def p_copy(k, e):
        return pltpu.make_async_remote_copy(
            src_ref=psend.at[e, k - 1], dst_ref=pbuf.at[k - 1, e],
            send_sem=ps_sem.at[k - 1, e], recv_sem=pr_sem.at[k - 1, e],
            device_id={"loop": minus(me, k)}, device_id_type=MESH,
        )

    def h_copy(k, e):
        return pltpu.make_async_remote_copy(
            src_ref=hbuf.at[e, 0], dst_ref=hbuf.at[e, k],
            send_sem=hs_sem.at[k - 1, e], recv_sem=hr_sem.at[k - 1, e],
            device_id={"loop": plus(me, k)}, device_id_type=MESH,
        )

    def r_copy(j, e):
        return pltpu.make_async_remote_copy(
            src_ref=fsend.at[e, minus(me, plus(hid, j))], dst_ref=rbuf.at[j - 1, e],
            send_sem=rs_sem.at[j - 1, e], recv_sem=rr_sem.at[j - 1, e],
            device_id={"hid": plus(hid, j)}, device_id_type=MESH,
        )

    def t_copy(e):
        return pltpu.make_async_remote_copy(
            src_ref=tsend.at[e], dst_ref=fin.at[e],
            send_sem=ts_sem.at[e], recv_sem=tr_sem.at[e],
            device_id={"loop": hid, "hid": me}, device_id_type=MESH,
        )

    for k in others:
        x_copy(k, hid).start()
    for k in others:
        x_copy(k, hid).wait_recv()
        for j in others:
            x_forward(k, j).start()

    for e in range(experts):
        w_copies[e].wait()

        @pl.when(hid != e)
        def _():
            for k in others:
                x_copy(k, e).wait_recv()

        part = lax.dot_general(
            xbuf[:, e].reshape(n * CAP, slab), w[e, 0:2].reshape(2 * share, slab),
            (((1,), (1,)), ((), ())), preferred_element_type=f32,
        )
        pown[e] = part[:CAP]
        psend[e] = part[CAP:].astype(SENT).reshape(n - 1, CAP, 2 * share)
        for k in others:
            p_copy(k, e).start()

    for e in range(experts):
        for k in others:
            p_copy(k, e).wait_recv()
        total = pown[e]
        for k in others:
            total = total + pbuf[k - 1, e].astype(f32)
        gate, up = total[:, :share], total[:, share:]
        col = factor_col[e * CAP:(e + 1) * CAP]
        hbuf[e, 0] = (col * (gate / (1.0 + jnp.exp(-gate))) * up).astype(bf16)
        for k in others:
            h_copy(k, e).start()

    for e in range(experts):
        for k in others:
            h_copy(k, e).wait_recv()
        fsend[e] = jnp.dot(
            hbuf[e].reshape(n * CAP, share), w[e, 2], preferred_element_type=f32
        ).reshape(n, CAP, slab)
        for j in others:
            r_copy(j, e).start()

    par = par_ref[...]
    family_t = jnp.where(r_i == c_i // NODES * NODES + par, 1.0, 0.0)
    family = jnp.transpose(family_t).astype(bf16)
    place = jnp.transpose(place_t).astype(bf16)

    for e in range(experts):
        for j in others:
            r_copy(j, e).wait_recv()
        total = fsend[e, minus(me, hid)]
        for j in others:
            total = total + rbuf[j - 1, e]

        @pl.when(on_diag)
        def _():
            fin[e] = total.astype(bf16)

        @pl.when(jnp.logical_not(on_diag))
        def _():
            tsend[e] = total.astype(bf16)
            t_copy(e).start()

    @pl.when(jnp.logical_not(on_diag))
    def _():
        for e in range(experts):
            t_copy(e).wait_recv()

    value = jnp.dot(place, fin[...].reshape(slots, slab), preferred_element_type=f32).astype(bf16)
    out_ref[...] = value
    pout_ref[...] = jnp.dot(family, value, preferred_element_type=f32).astype(bf16)

    for k in others:
        x_copy(k, hid).wait_send()
        for j in others:
            x_forward(k, j).wait_send()
        for e in range(experts):
            p_copy(k, e).wait_send()
            h_copy(k, e).wait_send()
            r_copy(k, e).wait_send()

    @pl.when(jnp.logical_not(on_diag))
    def _():
        for e in range(experts):
            t_copy(e).wait_send()


def compact(tokens, route_ids, router_weights, accepted, parents, expert_weights):
    n = lax.axis_size("loop")
    rows = tokens.shape[0]
    experts, _, share, slab = expert_weights.shape
    bf16, f32 = jnp.bfloat16, jnp.float32
    vmem = pl.BlockSpec(memory_space=pltpu.VMEM)
    dma = pltpu.SemaphoreType.DMA
    args = (
        route_ids.T, router_weights.T, accepted.reshape(1, rows), parents.reshape(1, rows),
        tokens, expert_weights,
    )
    return pl.pallas_call(
        functools.partial(moe_kernel, n),
        out_shape=[jax.ShapeDtypeStruct((rows, slab), bf16)] * 2,
        in_specs=[pl.BlockSpec(memory_space=pltpu.HBM)] * 6,
        out_specs=[vmem] * 2,
        scratch_shapes=[pltpu.VMEM(a.shape, a.dtype) for a in args] + [
            pltpu.VMEM((n - 1, experts, CAP, slab), bf16),
            pltpu.VMEM((n, experts, CAP, slab), bf16),
            pltpu.VMEM((experts, CAP, 2 * share), f32),
            pltpu.VMEM((experts, n - 1, CAP, 2 * share), SENT),
            pltpu.VMEM((n - 1, experts, CAP, 2 * share), SENT),
            pltpu.VMEM((experts, n, CAP, share), bf16),
            pltpu.VMEM((experts, n, CAP, slab), f32),
            pltpu.VMEM((n - 1, experts, CAP, slab), f32),
            pltpu.VMEM((experts, CAP, slab), bf16),
            pltpu.VMEM((experts, CAP, slab), bf16),
            dma((5,)), dma((experts,)),
            dma((n - 1,)), dma((n - 1, n - 1)), dma((n - 1, experts)),
            dma((n - 1, experts)), dma((n - 1, experts)),
            dma((n - 1, experts)), dma((n - 1, experts)),
            dma((n - 1, experts)), dma((n - 1, experts)),
            dma((experts,)), dma((experts,)),
        ],
        compiler_params=pltpu.CompilerParams(
            collective_id=0, has_side_effects=True, vmem_limit_bytes=40 << 20
        ),
    )(*args)


def shifted(value, axis, by):
    devices = lax.axis_size(axis)
    return lax.ppermute(value, axis, [(i, (i + by) % devices) for i in range(devices)])


def move_one(piece, phase_name):
    if phase_name == "proj":
        return shifted(piece, "loop", 1)
    return shifted(piece, "loop", 1)


def rotate(piece, start_value, add_piece, phase_name):
    n_loop = lax.axis_size("loop")
    own_index = lax.axis_index("loop")
    total = add_piece(start_value, piece, own_index)

    def turn_body(turn_no, carried):
        arrived = move_one(carried[0], phase_name)
        anchor = jnp.mod(own_index - turn_no, n_loop)
        return (arrived, add_piece(carried[1], arrived, anchor))

    carried = lax.fori_loop(1, n_loop, turn_body, (piece, total))
    return carried[1]


def general(tokens, route_ids, router_weights, accepted, parents, expert_weights):
    row_count = tokens.shape[0]
    model_width = tokens.shape[1]
    window_count = expert_weights.shape[0]
    hidden_share = expert_weights.shape[2]
    slab_width = expert_weights.shape[3]
    proj_weights = expert_weights[:, 0:2]
    down_weights = expert_weights[:, 2]
    matches = route_ids[:, :, None] == jnp.arange(window_count, dtype=jnp.int32)[None, None, :]
    live_rows = accepted > 0
    combine = jnp.where(
        live_rows[:, None],
        jnp.sum(jnp.where(matches, router_weights[:, :, None], 0.0), axis=1),
        0.0,
    )

    def proj_piece(total, piece, anchor):
        columns = lax.dynamic_slice_in_dim(tokens, anchor * slab_width, slab_width, 1)
        return total + jnp.einsum(
            "rd,etfd->retf", columns, piece, preferred_element_type=jnp.float32
        )

    proj_start = jnp.zeros((row_count, window_count, 2, hidden_share), jnp.float32)
    projected = rotate(proj_weights, proj_start, proj_piece, "proj")
    weighted = (combine[:, :, None] * jax.nn.silu(projected[:, :, 0]) * projected[:, :, 1]).astype(
        jnp.bfloat16
    )

    def down_piece(total, piece, anchor):
        block = jnp.einsum("ref,efd->rd", weighted, piece, preferred_element_type=jnp.float32)
        return lax.dynamic_update_slice_in_dim(total, block, anchor * slab_width, 1)

    partial_value = rotate(
        down_weights, jnp.zeros((row_count, model_width), jnp.float32), down_piece, "down"
    )
    share_width = model_width // lax.axis_size("hid")
    summed_all = lax.psum(partial_value, "hid")
    expert_out = lax.dynamic_slice_in_dim(
        summed_all, lax.axis_index("hid") * share_width, share_width, 1
    ).astype(jnp.bfloat16)
    tree_count = row_count // NODES
    family = jax.nn.one_hot(parents.reshape(tree_count, NODES), NODES, dtype=jnp.bfloat16)
    grouped = expert_out.reshape(tree_count, NODES, share_width)
    parent_out = jnp.einsum("qnm,qmd->qnd", family, grouped, preferred_element_type=jnp.float32)
    parent_out = parent_out.astype(jnp.bfloat16).reshape(row_count, share_width)
    return (expert_out, parent_out)


def local(tokens, route_ids, router_weights, accepted, parents, expert_weights):
    args = (tokens, route_ids, router_weights, accepted, parents, expert_weights)
    experts, _, share, slab = expert_weights.shape
    n_loop, n_hid = lax.axis_size("loop"), lax.axis_size("hid")
    if n_loop == n_hid and slab % 128 == 0 and share % 128 == 0 and experts == n_hid:
        return tuple(compact(*args))
    return general(*args)


def solution(mesh):
    in_specs = (
        P(("groups", "loop"), None),
        P(("groups", "loop"), None),
        P(("groups", "loop"), None),
        P(("groups", "loop")),
        P(("groups", "loop")),
        P(None, None, "hid", "loop"),
    )
    out_specs = (P(("groups", "loop"), "hid"), P(("groups", "loop"), "hid"))
    return jax.shard_map(local, mesh=mesh, in_specs=in_specs, out_specs=out_specs, check_vma=False)
```

time: 81.2 us -> 63.9 us (0.79)
  the two profiles are of different devices: /device:TPU:2 before, /device:TPU:3 now
where the time goes in v2:
time: 63.9 us; the launch traced here: 63.6 us
  Pallas kernels  55.2 us (86%)
  local copies, waits for them, and re-layouts  7.71 us (12%)
  between operations  0.65 us (1%)
    pallas_call x1, Pallas kernels, compact(): pl.pallas_call(functools.partial(moe_kernel, n), out_shape=[jax.ShapeDtyp...  55.2 us
    unnamed x14, local copies, waits for them, and re-layouts  7.71 us

profile of v2, /device:TPU:3, one launch (start us, length us, event | category | flops | bytes accessed | tf_op | source)
XLA Modules:
  0.0 63.6 jit_solution(7463972307726075160)
XLA Ops:
  0.6 0.0 copy-start
  0.6 2.3 %copy-done = bf16[4,3,384,512]{3,2,1,0:T(8,128)(2,1)S(1)} copy-done((bf16[4,3,384,512]{3,2,1,0:T(8,128)(2,1)S(1)}, bf16[4,3,384,512]{3,2,1,0:T(8,128)(2,1)}, u32[]{:S(2)}) %copy-start) | copy-done | bytes 4718616
  3.0 0.0 copy-start.1
  3.0 1.2 %copy-done.1 = bf16[256,2048]{1,0:T(8,128)(2,1)S(1)} copy-done((bf16[256,2048]{1,0:T(8,128)(2,1)S(1)}, bf16[256,2048]{1,0:T(8,128)(2,1)}, u32[]{:S(2)}) %copy-start.1) | copy-done | bytes 1048600
  4.2 0.0 copy-start.2
  4.2 0.7 %copy-done.2 = s32[256,8]{0,1:T(8,128)S(1)} copy-done((s32[256,8]{0,1:T(8,128)S(1)}, s32[256,8]{0,1:T(8,128)}, u32[]{:S(2)}) %copy-start.2) | copy-done | bytes 8216
  4.9 0.0 copy-start.3
  4.9 0.7 %copy-done.3 = f32[256,8]{0,1:T(8,128)S(1)} copy-done((f32[256,8]{0,1:T(8,128)S(1)}, f32[256,8]{0,1:T(8,128)}, u32[]{:S(2)}) %copy-start.3) | copy-done | bytes 8216
  5.6 0.0 copy-start.4
  5.6 0.7 %copy-done.4 = s32[256]{0:T(256)S(1)} copy-done((s32[256]{0:T(256)S(1)}, s32[256]{0:T(256)}, u32[]{:S(2)}) %copy-start.4) | copy-done | bytes 1048
  6.3 0.0 copy-start.5
  6.3 0.7 %copy-done.5 = s32[256]{0:T(256)S(1)} copy-done((s32[256]{0:T(256)S(1)}, s32[256]{0:T(256)}, u32[]{:S(2)}) %copy-start.5) | copy-done | bytes 1048
  6.9 55.2 %shard_map.77 = (bf16[256,512]{1,0:T(8,128)(2,1)S(1)}, bf16[256,512]{1,0:T(8,128)(2,1)S(1)}) custom-call(s32[8,256]{1,0:T(8,128)S(1)} %bitcast.4, f32[8,256]{1,0:T(8,128)S(1)} %bitcast.5, s32[1,256]{1,0:T(1,128)S(1)} %bitcast.6, s32[1,256]{1,0:T(1,128)S(1)} %bitcast.7, bf16[256,2048]{1,0:T(8,128)(2,1)S(1)} %copy-done.1, bf16[4,3,384,512]{3,2,1,0:T(8,128)(2,1)S(1)} %copy-done), custom_call_target="tpu_custom_call" | custom-call | tf_op jit(solution)/shard_map/pallas_call | solution.py:244
  62.2 0.7 %copy.10 = bf16[256,512]{1,0:T(8,128)(2,1)} copy(bf16[256,512]{1,0:T(8,128)(2,1)S(1)} %get-tuple-element.4) | data formatting | bytes 524288
  62.9 0.7 %copy.11 = bf16[256,512]{1,0:T(8,128)(2,1)} copy(bf16[256,512]{1,0:T(8,128)(2,1)S(1)} %get-tuple-element.5) | data formatting | bytes 524288
Async XLA Ops:
  0.6 2.3 %copy-start = (bf16[4,3,384,512]{3,2,1,0:T(8,128)(2,1)S(1)}, bf16[4,3,384,512]{3,2,1,0:T(8,128)(2,1)}, u32[]{:S(2)}) copy-start(bf16[4,3,384,512]{3,2,1,0:T(8,128)(2,1)} %w_hbm.1) | copy-start | bytes 14155780
  3.0 1.2 %copy-start.1 = (bf16[256,2048]{1,0:T(8,128)(2,1)S(1)}, bf16[256,2048]{1,0:T(8,128)(2,1)}, u32[]{:S(2)}) copy-start(bf16[256,2048]{1,0:T(8,128)(2,1)} %tok_hbm.1) | copy-start | bytes 3145732
  4.2 0.7 %copy-start.2 = (s32[256,8]{0,1:T(8,128)S(1)}, s32[256,8]{0,1:T(8,128)}, u32[]{:S(2)}) copy-start(s32[256,8]{0,1:T(8,128)} %param.7) | copy-start | bytes 24580
  4.9 0.7 %copy-start.3 = (f32[256,8]{0,1:T(8,128)S(1)}, f32[256,8]{0,1:T(8,128)}, u32[]{:S(2)}) copy-start(f32[256,8]{0,1:T(8,128)} %param.8) | copy-start | bytes 24580
  5.6 0.7 %copy-start.4 = (s32[256]{0:T(256)S(1)}, s32[256]{0:T(256)}, u32[]{:S(2)}) copy-start(s32[256]{0:T(256)} %param.9) | copy-start | bytes 3076
  6.3 0.7 %copy-start.5 = (s32[256]{0:T(256)S(1)}, s32[256]{0:T(256)}, u32[]{:S(2)}) copy-start(s32[256]{0:T(256)} %param.10) | copy-start | bytes 3076

commit v3 on v2

--- a/solution.py
+++ b/solution.py
@@ -147,7 +147,7 @@
         for j in others:
             x_forward(k, j).start()
 
-    for e in range(experts):
+    def project(e):
         w_copies[e].wait()
 
         @pl.when(hid != e)
@@ -164,7 +164,7 @@
         for k in others:
             p_copy(k, e).start()
 
-    for e in range(experts):
+    def activate(e):
         for k in others:
             p_copy(k, e).wait_recv()
         total = pown[e]
@@ -176,7 +176,7 @@
         for k in others:
             h_copy(k, e).start()
 
-    for e in range(experts):
+    def down(e):
         for k in others:
             h_copy(k, e).wait_recv()
         fsend[e] = jnp.dot(
@@ -185,26 +185,36 @@
         for j in others:
             r_copy(j, e).start()
 
+    def collect(e):
+        for j in others:
+            r_copy(j, e).wait_recv()
+        total = fsend[e, minus(me, hid)]
+        for j in others:
+            total = total + rbuf[j - 1, e]
+
+        @pl.when(on_diag)
+        def _():
+            fin[e] = total.astype(bf16)
+
+        @pl.when(jnp.logical_not(on_diag))
+        def _():
+            tsend[e] = total.astype(bf16)
+            t_copy(e).start()
+
+    project(0)
     par = par_ref[...]
     family_t = jnp.where(r_i == c_i // NODES * NODES + par, 1.0, 0.0)
     family = jnp.transpose(family_t).astype(bf16)
     place = jnp.transpose(place_t).astype(bf16)
-
-    for e in range(experts):
-        for j in others:
-            r_copy(j, e).wait_recv()
-        total = fsend[e, minus(me, hid)]
-        for j in others:
-            total = total + rbuf[j - 1, e]
-
-        @pl.when(on_diag)
-        def _():
-            fin[e] = total.astype(bf16)
-
-        @pl.when(jnp.logical_not(on_diag))
-        def _():
-            tsend[e] = total.astype(bf16)
-            t_copy(e).start()
+    for turn in range(experts + 2):
+        if turn + 1 < experts:
+            project(turn + 1)
+        if turn < experts:
+            activate(turn)
+        if 0 <= turn - 1 < experts:
+            down(turn - 1)
+        if 0 <= turn - 2 < experts:
+            collect(turn - 2)
 
     @pl.when(jnp.logical_not(on_diag))
     def _():
@@ -265,7 +275,7 @@
             dma((experts,)), dma((experts,)),
         ],
         compiler_params=pltpu.CompilerParams(
-            collective_id=0, has_side_effects=True, vmem_limit_bytes=40 << 20
+            collective_id=0, has_side_effects=True, vmem_limit_bytes=60 << 20
         ),
     )(*args)
 

time: 63.9 us -> 57.8 us (0.905)
  local copies, waits for them, and re-layouts: 7.71 us -> 3.34 us
  Pallas kernels: 55.2 us -> 53.1 us
    unnamed x14 -> x2, local copies, waits for them, and re-layouts: 7.71 us -> 3.34 us
    pallas_call x1, Pallas kernels: 55.2 us -> 53.1 us  [compact(): pl.pallas_call(functools.partial(moe_kernel, n), out_shape=[jax.ShapeDtyp...]
where the time goes in v3:
time: 57.8 us; the launch traced here: 57.1 us
  Pallas kernels  53.1 us (92%)
  local copies, waits for them, and re-layouts  3.34 us (6%)
  between operations  0.64 us (1%)
    pallas_call x1, Pallas kernels, compact(): pl.pallas_call(functools.partial(moe_kernel, n), out_shape=[jax.ShapeDtyp...  53.1 us
    unnamed x2, local copies, waits for them, and re-layouts  3.34 us

profile of v3, /device:TPU:3, one launch (start us, length us, event | category | flops | bytes accessed | tf_op | source)
XLA Modules:
  0.0 57.1 jit_solution(12308450937994287449)
XLA Ops:
  0.6 53.1 %shard_map.77 = (bf16[256,512]{1,0:T(8,128)(2,1)}, bf16[256,512]{1,0:T(8,128)(2,1)}) custom-call(s32[8,256]{1,0:T(8,128)} %bitcast.4, f32[8,256]{1,0:T(8,128)} %bitcast.5, s32[1,256]{1,0:T(1,128)} %bitcast.6, s32[1,256]{1,0:T(1,128)} %bitcast.7, bf16[256,2048]{1,0:T(8,128)(2,1)} %tok_hbm.1, bf16[4,3,384,512]{3,2,1,0:T(8,128)(2,1)} %w_hbm.1), custom_call_target="tpu_custom_call" | custom-call | tf_op jit(solution)/shard_map/pallas_call | solution.py:254
  53.7 1.7 %copy.10 = bf16[256,512]{1,0:T(8,128)(2,1)} copy(bf16[256,512]{1,0:T(8,128)(2,1)} %get-tuple-element.4) | data formatting | bytes 524288
  55.4 1.7 %copy.11 = bf16[256,512]{1,0:T(8,128)(2,1)} copy(bf16[256,512]{1,0:T(8,128)(2,1)} %get-tuple-element.5) | data formatting | bytes 524288

commit v4 on v3

--- a/solution.py
+++ b/solution.py
@@ -14,8 +14,8 @@
 
 
 def moe_kernel(
-    n, ids_hbm, rw_hbm, acc_hbm, par_hbm, tok_hbm, w_hbm, out_ref, pout_ref,
-    ids_ref, rw_ref, acc_ref, par_ref, tok_ref, w,
+    n, ids_hbm, rw_hbm, acc_hbm, tok_hbm, w_hbm, sums_ref, place_ref,
+    ids_ref, rw_ref, acc_ref, tok_ref, w,
     xsend, xbuf, pown, psend, pbuf, hbuf, fsend, rbuf, tsend, fin,
     in_sem, w_sem, xs_sem, xf_sem, xr_sem, ps_sem, pr_sem, hs_sem, hr_sem,
     rs_sem, rr_sem, ts_sem, tr_sem,
@@ -46,7 +46,7 @@
     inputs = [
         pltpu.make_async_copy(source, target, in_sem.at[i])
         for i, (source, target) in enumerate(
-            [(ids_hbm, ids_ref), (rw_hbm, rw_ref), (acc_hbm, acc_ref), (par_hbm, par_ref), (tok_hbm, tok_ref)]
+            [(ids_hbm, ids_ref), (rw_hbm, rw_ref), (acc_hbm, acc_ref), (tok_hbm, tok_ref)]
         )
     ]
     for copy in inputs:
@@ -148,21 +148,22 @@
             x_forward(k, j).start()
 
     def project(e):
-        w_copies[e].wait()
-
+        pltpu.make_async_copy(w_hbm.at[e], w.at[e], w_sem.at[e]).wait()
+        part = lax.dot_general(
+            xbuf[:, e].reshape(n * CAP, slab), w[e, 0:2].reshape(2 * share, slab),
+            (((1,), (1,)), ((), ())), preferred_element_type=f32,
+        )
+        pown[e] = part[:CAP]
+        psend[e] = part[CAP:].astype(SENT).reshape(n - 1, CAP, 2 * share)
+        for k in others:
+            p_copy(k, e).start()
+
+    def project_other(e):
         @pl.when(hid != e)
         def _():
             for k in others:
                 x_copy(k, e).wait_recv()
-
-        part = lax.dot_general(
-            xbuf[:, e].reshape(n * CAP, slab), w[e, 0:2].reshape(2 * share, slab),
-            (((1,), (1,)), ((), ())), preferred_element_type=f32,
-        )
-        pown[e] = part[:CAP]
-        psend[e] = part[CAP:].astype(SENT).reshape(n - 1, CAP, 2 * share)
-        for k in others:
-            p_copy(k, e).start()
+            project(e)
 
     def activate(e):
         for k in others:
@@ -201,14 +202,12 @@
             tsend[e] = total.astype(bf16)
             t_copy(e).start()
 
-    project(0)
-    par = par_ref[...]
-    family_t = jnp.where(r_i == c_i // NODES * NODES + par, 1.0, 0.0)
-    family = jnp.transpose(family_t).astype(bf16)
-    place = jnp.transpose(place_t).astype(bf16)
+    project(hid)
+    project_other(0)
+    place_ref[...] = jnp.transpose(place_t).astype(bf16)
     for turn in range(experts + 2):
         if turn + 1 < experts:
-            project(turn + 1)
+            project_other(turn + 1)
         if turn < experts:
             activate(turn)
         if 0 <= turn - 1 < experts:
@@ -221,9 +220,7 @@
         for e in range(experts):
             t_copy(e).wait_recv()
 
-    value = jnp.dot(place, fin[...].reshape(slots, slab), preferred_element_type=f32).astype(bf16)
-    out_ref[...] = value
-    pout_ref[...] = jnp.dot(family, value, preferred_element_type=f32).astype(bf16)
+    sums_ref[...] = fin[...].reshape(slots, slab)
 
     for k in others:
         x_copy(k, hid).wait_send()
@@ -238,6 +235,18 @@
     def _():
         for e in range(experts):
             t_copy(e).wait_send()
+
+
+def rows_kernel(sums_ref, place_ref, par_ref, out_ref, pout_ref):
+    rows = place_ref.shape[0]
+    f32, bf16 = jnp.float32, jnp.bfloat16
+    r_i = lax.broadcasted_iota(jnp.int32, (rows, rows), 0)
+    c_i = lax.broadcasted_iota(jnp.int32, (rows, rows), 1)
+    family_t = jnp.where(r_i == c_i // NODES * NODES + par_ref[...], 1.0, 0.0)
+    family = jnp.transpose(family_t).astype(bf16)
+    value = jnp.dot(place_ref[...], sums_ref[...], preferred_element_type=f32).astype(bf16)
+    out_ref[...] = value
+    pout_ref[...] = jnp.dot(family, value, preferred_element_type=f32).astype(bf16)
 
 
 def compact(tokens, route_ids, router_weights, accepted, parents, expert_weights):
@@ -248,13 +257,16 @@
     vmem = pl.BlockSpec(memory_space=pltpu.VMEM)
     dma = pltpu.SemaphoreType.DMA
     args = (
-        route_ids.T, router_weights.T, accepted.reshape(1, rows), parents.reshape(1, rows),
+        route_ids.T, router_weights.T, accepted.reshape(1, rows),
         tokens, expert_weights,
     )
-    return pl.pallas_call(
+    sums, place = pl.pallas_call(
         functools.partial(moe_kernel, n),
-        out_shape=[jax.ShapeDtypeStruct((rows, slab), bf16)] * 2,
-        in_specs=[pl.BlockSpec(memory_space=pltpu.HBM)] * 6,
+        out_shape=[
+            jax.ShapeDtypeStruct((experts * CAP, slab), bf16),
+            jax.ShapeDtypeStruct((rows, experts * CAP), bf16),
+        ],
+        in_specs=[pl.BlockSpec(memory_space=pltpu.HBM)] * 5,
         out_specs=[vmem] * 2,
         scratch_shapes=[pltpu.VMEM(a.shape, a.dtype) for a in args] + [
             pltpu.VMEM((n - 1, experts, CAP, slab), bf16),
@@ -267,7 +279,7 @@
             pltpu.VMEM((n - 1, experts, CAP, slab), f32),
             pltpu.VMEM((experts, CAP, slab), bf16),
             pltpu.VMEM((experts, CAP, slab), bf16),
-            dma((5,)), dma((experts,)),
+            dma((4,)), dma((experts,)),
             dma((n - 1,)), dma((n - 1, n - 1)), dma((n - 1, experts)),
             dma((n - 1, experts)), dma((n - 1, experts)),
             dma((n - 1, experts)), dma((n - 1, experts)),
@@ -278,6 +290,12 @@
             collective_id=0, has_side_effects=True, vmem_limit_bytes=60 << 20
         ),
     )(*args)
+    return pl.pallas_call(
+        rows_kernel,
+        out_shape=[jax.ShapeDtypeStruct((rows, slab), bf16)] * 2,
+        in_specs=[vmem] * 3,
+        out_specs=[vmem] * 2,
+    )(sums, place, parents.reshape(1, rows))
 
 
 def shifted(value, axis, by):

time: 57.8 us -> 52.9 us (0.915)
  local copies, waits for them, and re-layouts: 3.34 us -> 0 us
  Pallas kernels: 53.1 us -> 52.1 us
    unnamed x2 -> x0, local copies, waits for them, and re-layouts: 3.34 us -> none
    pallas_call x1, Pallas kernels: 53.1 us -> 50 us  [compact(): pl.pallas_call(functools.partial(moe_kernel, n), out_shape=[jax.ShapeDtyp...]
    pallas_call x0 -> x1, Pallas kernels: none -> 2.06 us  [compact(): pl.pallas_call(rows_kernel, out_shape=[jax.ShapeDtypeStruct((rows, slab),...]
where the time goes in v4:
time: 52.9 us; the launch traced here: 52.7 us
  Pallas kernels  52.1 us (98%)
  between operations  0.64 us (1%)
    pallas_call x1, Pallas kernels, compact(): pl.pallas_call(functools.partial(moe_kernel, n), out_shape=[jax.ShapeDtyp...  50 us
    pallas_call x1, Pallas kernels, compact(): pl.pallas_call(rows_kernel, out_shape=[jax.ShapeDtypeStruct((rows, slab),...  2.06 us

profile of v4, /device:TPU:3, one launch (start us, length us, event | category | flops | bytes accessed | tf_op | source)
XLA Modules:
  0.0 52.7 jit_solution(7950090390683074772)
XLA Ops:
  0.6 50.0 %shard_map.77 = (bf16[128,512]{1,0:T(8,128)(2,1)}, bf16[256,128]{1,0:T(8,128)(2,1)}) custom-call(s32[8,256]{1,0:T(8,128)} %bitcast.4, f32[8,256]{1,0:T(8,128)} %bitcast.5, s32[1,256]{1,0:T(1,128)} %bitcast.6, bf16[256,2048]{1,0:T(8,128)(2,1)} %tok_hbm.1, bf16[4,3,384,512]{3,2,1,0:T(8,128)(2,1)} %w_hbm.1), custom_call_target="tpu_custom_call" | custom-call | tf_op jit(solution)/shard_map/pallas_call | solution.py:263
  50.6 2.1 %shard_map.78 = (bf16[256,512]{1,0:T(8,128)(2,1)}, bf16[256,512]{1,0:T(8,128)(2,1)}) custom-call(bf16[128,512]{1,0:T(8,128)(2,1)} %get-tuple-element.4.sums_ref, bf16[256,128]{1,0:T(8,128)(2,1)} %get-tuple-element.5.place_ref, s32[1,256]{1,0:T(1,128)} %bitcast.7), custom_call_target="tpu_custom_call" | custom-call | tf_op jit(solution)/shard_map/pallas_call | solution.py:293

commit v5 on v4

--- a/solution.py
+++ b/solution.py
@@ -155,7 +155,7 @@
         )
         pown[e] = part[:CAP]
         psend[e] = part[CAP:].astype(SENT).reshape(n - 1, CAP, 2 * share)
-        for k in others:
+        for k in others[1:] + others[:1]:
             p_copy(k, e).start()
 
     def project_other(e):
@@ -204,10 +204,11 @@
 
     project(hid)
     project_other(0)
+    project_other(1)
     place_ref[...] = jnp.transpose(place_t).astype(bf16)
     for turn in range(experts + 2):
-        if turn + 1 < experts:
-            project_other(turn + 1)
+        if turn + 2 < experts:
+            project_other(turn + 2)
         if turn < experts:
             activate(turn)
         if 0 <= turn - 1 < experts:

time: 52.9 us -> 51.5 us (0.974)
  Pallas kernels: 52.1 us -> 50.7 us
    pallas_call x1, Pallas kernels: 50 us -> 48.6 us  [compact(): pl.pallas_call(functools.partial(moe_kernel, n), out_shape=[jax.ShapeDtyp...]
where the time goes in v5:
time: 51.5 us; the launch traced here: 51.3 us
  Pallas kernels  50.7 us (98%)
  between operations  0.64 us (1%)
    pallas_call x1, Pallas kernels, compact(): pl.pallas_call(functools.partial(moe_kernel, n), out_shape=[jax.ShapeDtyp...  48.6 us
    pallas_call x1, Pallas kernels, compact(): pl.pallas_call(rows_kernel, out_shape=[jax.ShapeDtypeStruct((rows, slab),...  2.06 us

profile of v5, /device:TPU:3, one launch (start us, length us, event | category | flops | bytes accessed | tf_op | source)
XLA Modules:
  0.0 51.3 jit_solution(16836641771796671835)
XLA Ops:
  0.6 48.6 %shard_map.77 = (bf16[128,512]{1,0:T(8,128)(2,1)}, bf16[256,128]{1,0:T(8,128)(2,1)}) custom-call(s32[8,256]{1,0:T(8,128)} %bitcast.4, f32[8,256]{1,0:T(8,128)} %bitcast.5, s32[1,256]{1,0:T(1,128)} %bitcast.6, bf16[256,2048]{1,0:T(8,128)(2,1)} %tok_hbm.1, bf16[4,3,384,512]{3,2,1,0:T(8,128)(2,1)} %w_hbm.1), custom_call_target="tpu_custom_call" | custom-call | tf_op jit(solution)/shard_map/pallas_call | solution.py:264
  49.3 2.1 %shard_map.78 = (bf16[256,512]{1,0:T(8,128)(2,1)}, bf16[256,512]{1,0:T(8,128)(2,1)}) custom-call(bf16[128,512]{1,0:T(8,128)(2,1)} %get-tuple-element.4.sums_ref, bf16[256,128]{1,0:T(8,128)(2,1)} %get-tuple-element.5.place_ref, s32[1,256]{1,0:T(1,128)} %bitcast.7), custom_call_target="tpu_custom_call" | custom-call | tf_op jit(solution)/shard_map/pallas_call | solution.py:294
